TPU v7x, 32 devices: a whole 2x2x4 slice. The times are simulated.
32 devices in a mesh: region: 4 (over x, core), dom: 8 (over z, y).
Axes of the slice: x: 2, y: 2, z: 4, core: 2. Of those that a mesh axis runs over, the one named last changes fastest.
Arguments:
- fine_latents: bfloat16 [65536, 256], P(('region', 'dom')), may hold values from -6 to 6
- edge_latents: bfloat16 [294912, 256], P(('region', 'dom')), may hold values from -6 to 6
- send_rows: int32 [8192], P(('region', 'dom')), may hold values from 0 to 2047
- edge_senders: int32 [294912], P(('region', 'dom')), may hold values from 0 to 2303
- edge_targets: int32 [294912], P(('region', 'dom')), may hold values from 0 to 2047
- cluster_ids: int32 [65536], P(('region', 'dom')), may hold values from 0 to 1023, as said below
- coarse_latents: bfloat16 [1024, 256], P(('region', 'dom')), may hold values from -6 to 6
- coarse_senders: int32 [16384], P(('region', 'dom')), may hold values from 0 to 1023, as said below
- coarse_targets: int32 [16384], P(('region', 'dom')), may hold values from 0 to 1023, as said below
- sender_weight: bfloat16 [256, 256], replicated, may hold values from -0.375 to 0.375
- target_weight: bfloat16 [256, 256], replicated, may hold values from -0.375 to 0.375
- edge_weight: bfloat16 [256, 256], replicated, may hold values from -0.375 to 0.375
- message_weight: bfloat16 [256, 256], replicated, may hold values from -0.375 to 0.375
- self_weight: bfloat16 [256, 256], replicated, may hold values from -0.375 to 0.375
- inflow_weight: bfloat16 [256, 256], replicated, may hold values from -0.375 to 0.375
- update_weight: bfloat16 [256, 256], replicated, may hold values from -0.375 to 0.375
- pooling_weight: bfloat16 [256, 256], replicated, may hold values from -0.046875 to 0.046875
- upper_sender: bfloat16 [256, 256], replicated, may hold values from -0.375 to 0.375
- upper_target: bfloat16 [256, 256], replicated, may hold values from -0.375 to 0.375
- upper_update: bfloat16 [256, 256], replicated, may hold values from -0.375 to 0.375
- lifting_weight: bfloat16 [256, 256], replicated, may hold values from -0.375 to 0.375
Outputs:
- fine_out: bfloat16 [65536, 256], P(('region', 'dom'))
- coarse_out: bfloat16 [1024, 256], P(('region', 'dom'))
Inputs may be any that keep to these rules, and one draw needn't show every extreme that they name: `cluster_ids`: A fine node of partition p in region r has its coarse node in region r's block (r * 256 to (r + 1) * 256 - 1) or in the block of region (r + 2) modulo 4; cluster sizes are uneven. `coarse_senders`: the sender of a coarse edge held by device p of region r lies in region r's block of 256 coarse nodes. `coarse_targets`: the target of a coarse edge held by device p lies in p's own 32 coarse nodes, p * 32 to (p + 1) * 32 - 1.
All inputs are finite; a program needn't handle non-finite values.
Results may differ from a plain program's by a relative error of at most 0.0095.
Values may be sent and summed in bfloat16 or wider, within the bound.
A program may use at most 128 MiB of HBM per device.

v0:
```python
import jax
import jax.numpy as jnp
from jax import lax
from jax.sharding import PartitionSpec as P


def with_halo(cells, sides, width):
    for axis, dim in sides:
        count = lax.axis_size(axis)
        ends = count - 1
        head = lax.slice_in_dim(cells, 0, width, axis=dim)
        tail = lax.slice_in_dim(cells, cells.shape[dim] - width, cells.shape[dim], axis=dim)
        cells = jnp.concatenate(
            [
                lax.ppermute(tail, axis, [(i, (i + 1) % count) for i in range(ends)]),
                cells,
                lax.ppermute(head, axis, [((i + 1) % count, i) for i in range(ends)]),
            ],
            axis=dim,
        )
    return cells


def passed_along(value, axis, by):
    size = lax.axis_size(axis)
    return lax.ppermute(value, axis, [(i, (i + by) % size) for i in range(size)])


def normalize(values):
    centered = values - jnp.mean(values, axis=-1, keepdims=True)
    variance = jnp.mean(centered * centered, axis=-1, keepdims=True)
    return centered * lax.rsqrt(variance + 1e-05)


def body(
    fine_latents,
    edge_latents,
    send_rows,
    edge_senders,
    edge_targets,
    cluster_ids,
    coarse_latents,
    coarse_senders,
    coarse_targets,
    sender_weight,
    target_weight,
    edge_weight,
    message_weight,
    self_weight,
    inflow_weight,
    update_weight,
    pooling_weight,
    upper_sender,
    upper_target,
    upper_update,
    lifting_weight,
):
    node_count = fine_latents.shape[0]
    halo_width = send_rows.shape[0] // 2
    exported = jnp.take(fine_latents, send_rows, axis=0)
    widened = with_halo(exported, (("dom", 0),), halo_width)
    to_side = jnp.dot(fine_latents, target_weight, preferred_element_type=jnp.float32).astype(
        jnp.bfloat16
    )
    edge_part = jnp.dot(edge_latents, edge_weight, preferred_element_type=jnp.float32)
    extended = jnp.concatenate(
        [fine_latents, widened[:halo_width], widened[3 * halo_width :]], axis=0
    )
    from_side = jnp.dot(extended, sender_weight, preferred_element_type=jnp.float32).astype(
        jnp.bfloat16
    )
    preact = jnp.take(from_side, edge_senders, axis=0).astype(jnp.float32) + jnp.take(
        to_side, edge_targets, axis=0
    ).astype(jnp.float32)
    hidden = jax.nn.silu(preact + edge_part).astype(jnp.bfloat16)
    message = normalize(jnp.dot(hidden, message_weight, preferred_element_type=jnp.float32)).astype(
        jnp.bfloat16
    )
    inflow = jax.ops.segment_sum(
        message.astype(jnp.float32), edge_targets, num_segments=node_count
    ).astype(jnp.bfloat16)
    node_hidden = jnp.dot(fine_latents, self_weight, preferred_element_type=jnp.float32) + jnp.dot(
        inflow, inflow_weight, preferred_element_type=jnp.float32
    )
    node_hidden = jax.nn.silu(node_hidden).astype(jnp.bfloat16)
    refined = (
        fine_latents.astype(jnp.float32)
        + normalize(jnp.dot(node_hidden, update_weight, preferred_element_type=jnp.float32))
    ).astype(jnp.bfloat16)
    region_index = lax.axis_index("region")
    dom_index = lax.axis_index("dom")
    dom_count = lax.axis_size("dom")
    partner_step = lax.axis_size("region") // 2
    owned = coarse_latents.shape[0]
    region_block = dom_count * owned
    cluster_region = cluster_ids // region_block
    is_partner = (cluster_region != region_index).astype(jnp.int32)
    window_ids = cluster_ids % region_block + is_partner * region_block
    refined_wide = refined.astype(jnp.float32)
    number = lax.axis_size(("region", "dom")) * owned
    inside = (cluster_ids >= 0) & (cluster_ids < number)
    slot_ids = jnp.where(inside, cluster_ids, number)
    summed = jax.ops.segment_sum(refined_wide, slot_ids, num_segments=number + 1)
    pooled_sum = lax.psum_scatter(
        summed[:number], ("region", "dom"), scatter_dimension=0, tiled=True
    )
    pooled = pooled_sum.astype(jnp.bfloat16)
    coarse_start = (
        coarse_latents.astype(jnp.float32)
        + jnp.dot(pooled, pooling_weight, preferred_element_type=jnp.float32)
    ).astype(jnp.bfloat16)
    upper_from = jnp.dot(coarse_start, upper_sender, preferred_element_type=jnp.float32).astype(
        jnp.bfloat16
    )
    upper_to = jnp.dot(coarse_start, upper_target, preferred_element_type=jnp.float32).astype(
        jnp.bfloat16
    )
    region_from = lax.all_gather(upper_from, "dom", axis=0, tiled=True)
    sender_slots = coarse_senders - region_index * region_block
    target_slots = coarse_targets - (region_index * dom_count + dom_index) * owned
    coarse_pre = jnp.take(region_from, sender_slots, axis=0).astype(jnp.float32) + jnp.take(
        upper_to, target_slots, axis=0
    ).astype(jnp.float32)
    coarse_message = jax.nn.silu(coarse_pre).astype(jnp.bfloat16)
    coarse_inflow = jax.ops.segment_sum(
        coarse_message.astype(jnp.float32), target_slots, num_segments=owned
    ).astype(jnp.bfloat16)
    coarse_update = normalize(
        jnp.dot(coarse_inflow, upper_update, preferred_element_type=jnp.float32)
    )
    coarse_out = (coarse_start.astype(jnp.float32) + coarse_update).astype(jnp.bfloat16)
    lifted = jnp.dot(coarse_out, lifting_weight, preferred_element_type=jnp.float32).astype(
        jnp.bfloat16
    )
    region_lifted = lax.all_gather(lifted, "dom", axis=0, tiled=True)
    partner_lifted = passed_along(region_lifted, "region", partner_step)
    window_lifted = jnp.concatenate([region_lifted, partner_lifted], axis=0)
    fine_out = (
        refined.astype(jnp.float32)
        + jnp.take(window_lifted, window_ids, axis=0).astype(jnp.float32)
    ).astype(jnp.bfloat16)
    return (fine_out, coarse_out)


def solution(mesh):
    return jax.shard_map(
        body,
        mesh=mesh,
        in_specs=(
            P(("region", "dom"), None),
            P(("region", "dom"), None),
            P(("region", "dom")),
            P(("region", "dom")),
            P(("region", "dom")),
            P(("region", "dom")),
            P(("region", "dom"), None),
            P(("region", "dom")),
            P(("region", "dom")),
            P(),
            P(),
            P(),
            P(),
            P(),
            P(),
            P(),
            P(),
            P(),
            P(),
            P(),
            P(),
        ),
        out_specs=(P(("region", "dom"), None), P(("region", "dom"), None)),
        check_vma=False,
    )
```

profile of v0, /device:TPU:0, one launch (start us, length us, event | category | flops | bytes accessed | tf_op | source)
XLA Modules:
  0.0 441.0 jit_solution(1961053075122461520)
XLA Ops:
  8.7 2.3 gather_fusion
  11.8 5.5 %collective-permute-start = (bf16[128,256]{1,0:T(8,128)(2,1)}, bf16[128,256]{1,0:T(8,128)(2,1)}, u32[]{:S(2)}, u32[]{:S(2)}) collective-permute-start(bf16[128,256]{1,0:T(8,128)(2,1)} %get-tuple-element.12), channel_id=1, source_target_pairs={{0,1},{1,2},{2,3},{3,4},{4,5},{5,6},{6,7},{8,9},{9,10},{10,11},{11... | collective-permute-start | bytes 196616 | tf_op jit(solution)/shard_map/ppermute | solution.py:15
  22.3 1.7 fusion.43
  25.3 36.9 %gather_fusion.2 = bf16[9216,256]{1,0:T(8,128)(2,1)} fusion(bf16[2048,256]{1,0:T(8,128)(2,1)S(1)} %convolution_convert_fusion.1, s32[9216]{0:T(1024)S(1)} %fusion.22), kind=kCustom, calls=%fused_computation.2 | custom fusion | bytes 9474048 | tf_op jit(solution)/shard_map/jit(_take)/gather | solution.py:72
  62.2 1.4 convolution_convert_fusion
  63.7 36.9 %gather_fusion.1 = bf16[9216,256]{1,0:T(8,128)(2,1)} fusion(bf16[2304,256]{1,0:T(8,128)(2,1)S(1)} %convolution_convert_fusion, s32[9216]{0:T(1024)S(1)} %fusion.21), kind=kCustom, calls=%fused_computation.1 | custom fusion | bytes 9474048 | tf_op jit(solution)/shard_map/jit(_take)/gather | solution.py:72
  100.5 12.1 %fusion.38 = (f32[9216]{0:T(1024)S(1)}, f32[9216,256]{0,1:T(8,128)}) fusion(bf16[256,256]{1,0:T(8,128)(2,1)S(1)} %copy-done, bf16[9216,256]{1,0:T(8,128)(2,1)} %param.22, bf16[256,256]{1,0:T(8,128)(2,1)S(1)} %copy-done.11, bf16[9216,256]{1,0:T(8,128)(2,1)} %gather_fusion.2, bf16[9216,256]{1,0:T(8,128)(2,1)} %gather_fusion.1, ...), kind=kOutput, calls=%fused_computation.96 | convolution fusion | flops 2444221440 | bytes 23910400 | tf_op jit(solution)/shard_map/dot_general | solution.py:76
  112.7 4.9 %multiply_reduce_fusion = f32[9216]{0:T(1024)S(1)} fusion(f32[9216,256]{0,1:T(8,128)} %get-tuple-element.15, f32[9216]{0:T(1024)S(1)} %broadcast_multiply_fusion), kind=kLoop, calls=%fused_computation.11 | loop fusion | flops 7068672 | bytes 9510912 | tf_op jit(solution)/shard_map/reduce_sum | solution.py:31
  117.6 1.4 copy-done.1
  119.0 4.9 %fusion = f32[9216,256]{0,1:T(8,128)} fusion(f32[9216,256]{0,1:T(8,128)S(1)} %copy-done.1, f32[9216]{0:T(1024)S(1)} %add_rsqrt_fusion, f32[9216]{0:T(1024)S(1)} %broadcast_multiply_fusion), kind=kLoop, calls=%fused_computation.13 | loop fusion | flops 9437184 | bytes 18948096 | tf_op jit(solution)/shard_map/convert_element_type | solution.py:80
  123.9 9.7 %copy.27 = f32[9216,256]{1,0:T(8,128)} copy(f32[9216,256]{0,1:T(8,128)} %fusion) | data formatting | bytes 18874368 | tf_op jit(solution)/shard_map/convert_element_type | solution.py:80
  133.6 51.4 %scatter_custom_fusion = f32[2048,256]{1,0:T(8,128)} fusion(s32[9216]{0:T(1024)} %param.25, f32[9216,256]{1,0:T(8,128)} %copy.27, f32[]{:T(128)} %constant.129.clone.1), kind=kCustom, calls=%fused_computation.37 | custom fusion | flops 2359296 | bytes 2097664 | tf_op jit(solution)/shard_map/scatter-add | solution.py:79
  185.0 3.2 fusion.39
  189.6 1.9 fusion.10
  191.5 1.9 copy.28
  193.4 12.2 %scatter_custom_fusion.1 = f32[1025,256]{1,0:T(8,128)S(1)} fusion(s32[2048]{0:T(1024)} %and_select_fusion, f32[2048,256]{1,0:T(8,128)} %copy.28, f32[]{:T(128)} %constant.129.clone.1), kind=kCustom, calls=%fused_computation.39 | custom fusion | flops 524288 | bytes 1050112 | tf_op jit(solution)/shard_map/scatter-add | solution.py:103
  208.7 135.8 %reduce-scatter.2.cloned.1.call-done = f32[32,256]{1,0:T(8,128)} async-done(((f32[1024,256]{1,0:T(8,128)}), f32[32,256]{1,0:T(8,128)}) %reduce-scatter.2.cloned.1.call-update) | async-done | bytes 32784 | tf_op jit(solution)/shard_map/reduce_scatter | solution.py:104
  345.7 30.5 %all_gather.6 = bf16[256,256]{1,0:T(8,128)(2,1)S(1)} all-gather(bf16[32,256]{1,0:T(8,128)(2,1)S(1)} %convolution_convert_fusion.4), channel_id=1, replica_groups=mesh['region'=4,'dom'=8] {'dom'}, dimensions={0}, use_global_device_ids=true | all-gather | bytes 147456 | tf_op jit(solution)/shard_map/all_gather | solution.py:118
  376.4 6.5 %scatter_custom_fusion.2 = f32[32,256]{1,0:T(8,128)S(1)} fusion(s32[512]{0:T(512)S(1)} %get-tuple-element.9, f32[]{:T(128)} %constant.136.clone.1, pred[512]{0:T(512)(128)(4,1)S(1)} %compare_and_fusion.3, pred[512]{0:T(512)(128)(4,1)S(1)} %get-tuple-element.10, bf16[]{:T(256)} %constant.135.clone.1, f32[]{:T(128)} %constant.129.clone.1, ...), kind=kCustom, calls=%fused_computation.41 | custom fusion | flops 1572864 | bytes 189450 | tf_op jit(solution)/shard_map/scatter-add | solution.py:125
  384.5 30.5 %all_gather.7 = bf16[256,256]{1,0:T(8,128)(2,1)S(1)} all-gather(bf16[32,256]{1,0:T(8,128)(2,1)S(1)} %convolution_convert_fusion.2), channel_id=1, replica_groups=mesh['region'=4,'dom'=8] {'dom'}, dimensions={0}, use_global_device_ids=true | all-gather | bytes 147456 | tf_op jit(solution)/shard_map/all_gather | solution.py:135
  415.4 4.6 %collective-permute-done.2 = bf16[256,256]{1,0:T(8,128)(2,1)S(1)} collective-permute-done((bf16[256,256]{1,0:T(8,128)(2,1)S(1)}, bf16[256,256]{1,0:T(8,128)(2,1)S(1)}, u32[]{:S(2)}, u32[]{:S(2)}) %collective-permute-start.2) | collective-permute-done | bytes 131104 | tf_op jit(solution)/shard_map/ppermute | solution.py:26
  420.0 9.1 %gather_fusion.3 = bf16[2048,256]{1,0:T(8,128)(2,1)} fusion(bf16[512,256]{1,0:T(8,128)(2,1)S(1)} %pad_maximum_fusion, s32[2048]{0:T(1024)S(1)} %broadcast_clamp_fusion), kind=kCustom, calls=%fused_computation.5 | custom fusion | bytes 2105344 | tf_op jit(solution)/shard_map/jit(_take)/gather | solution.py:140
  429.0 1.5 copy.29
  431.9 2.3 copy.30
  (65 shorter events, 17.6 us)
Async XLA Ops:
  7.2 93.4 %copy-start = (bf16[256,256]{1,0:T(8,128)(2,1)S(1)}, bf16[256,256]{1,0:T(8,128)(2,1)}, u32[]{:S(2)}) copy-start(bf16[256,256]{1,0:T(8,128)(2,1)} %param.33) | copy-start | bytes 393220
  7.2 13.8 %copy-start.2 = (bf16[2048,256]{1,0:T(8,128)(2,1)S(1)}, bf16[2048,256]{1,0:T(8,128)(2,1)}, u32[]{:S(2)}) copy-start(bf16[2048,256]{1,0:T(8,128)(2,1)} %param.21) | copy-start | bytes 3145732
  7.2 15.1 %copy-start.4 = (bf16[256,256]{1,0:T(8,128)(2,1)S(1)}, bf16[256,256]{1,0:T(8,128)(2,1)}, u32[]{:S(2)}) copy-start(bf16[256,256]{1,0:T(8,128)(2,1)} %param.34) | copy-start | bytes 393220
  7.2 337.3 %reduce-scatter.2.cloned.1.call-start = ((), (), s32[]{:S(2)}) async-start(), calls=%async_computation.1 | async-start | bytes 1081344 | tf_op jit(solution)/shard_map/reduce_scatter | solution.py:104
  11.8 50.4 %collective-permute-start = (bf16[128,256]{1,0:T(8,128)(2,1)}, bf16[128,256]{1,0:T(8,128)(2,1)}, u32[]{:S(2)}, u32[]{:S(2)}) collective-permute-start(bf16[128,256]{1,0:T(8,128)(2,1)} %get-tuple-element.12), channel_id=1, source_target_pairs={{0,1},{1,2},{2,3},{3,4},{4,5},{5,6},{6,7},{8,9},{9,10},{10,11},{11... | collective-permute-start | bytes 196616 | tf_op jit(solution)/shard_map/ppermute | solution.py:15
  17.3 44.9 %collective-permute-start.1 = (bf16[128,256]{1,0:T(8,128)(2,1)S(1)}, bf16[128,256]{1,0:T(8,128)(2,1)}, u32[]{:S(2)}, u32[]{:S(2)}) collective-permute-start(bf16[128,256]{1,0:T(8,128)(2,1)S(1)} %get-tuple-element.13), channel_id=1, source_target_pairs={{1,0},{2,1},{3,2},{4,3},{5,4},{6,5},{7,6},{9,8},{10,9},{11,10},{12... | collective-permute-start | bytes 196616 | tf_op jit(solution)/shard_map/ppermute | solution.py:17
  21.0 3.1 copy-start.9
  63.6 36.9 %copy-start.11 = (bf16[256,256]{1,0:T(8,128)(2,1)S(1)}, bf16[256,256]{1,0:T(8,128)(2,1)}, u32[]{:S(2)}) copy-start(bf16[256,256]{1,0:T(8,128)(2,1)} %param.32) | copy-start | bytes 393220
  112.7 6.4 %copy-start.1 = (f32[9216,256]{0,1:T(8,128)S(1)}, f32[9216,256]{0,1:T(8,128)}, u32[]{:S(2)}) copy-start(f32[9216,256]{0,1:T(8,128)} %get-tuple-element.15) | copy-start | bytes 28311556
  123.9 61.1 %copy-start.12 = (bf16[256,256]{1,0:T(8,128)(2,1)S(1)}, bf16[256,256]{1,0:T(8,128)(2,1)}, u32[]{:S(2)}) copy-start(bf16[256,256]{1,0:T(8,128)(2,1)} %param.36) | copy-start | bytes 393220
  188.2 1.4 copy-start.3
  193.4 152.2 %copy-start.5 = (bf16[256,256]{1,0:T(8,128)(2,1)S(1)}, bf16[256,256]{1,0:T(8,128)(2,1)}, u32[]{:S(2)}) copy-start(bf16[256,256]{1,0:T(8,128)(2,1)} %param.38) | copy-start | bytes 393220
  193.4 182.9 %copy-start.6 = (bf16[256,256]{1,0:T(8,128)(2,1)S(1)}, bf16[256,256]{1,0:T(8,128)(2,1)}, u32[]{:S(2)}) copy-start(bf16[256,256]{1,0:T(8,128)(2,1)} %param.39) | copy-start | bytes 393220
  206.7 177.7 %copy-start.7 = (bf16[256,256]{1,0:T(8,128)(2,1)S(1)}, bf16[256,256]{1,0:T(8,128)(2,1)}, u32[]{:S(2)}) copy-start(bf16[256,256]{1,0:T(8,128)(2,1)} %param.41) | copy-start | bytes 393220
  384.3 44.7 %copy-start.8 = (bf16[32,256]{1,0:T(8,128)(2,1)}, bf16[32,256]{1,0:T(8,128)(2,1)S(1)}, u32[]{:S(2)}) copy-start(bf16[32,256]{1,0:T(8,128)(2,1)S(1)} %add_convert_fusion.2) | copy-start | bytes 49156
  415.0 5.0 %collective-permute-start.2 = (bf16[256,256]{1,0:T(8,128)(2,1)S(1)}, bf16[256,256]{1,0:T(8,128)(2,1)S(1)}, u32[]{:S(2)}, u32[]{:S(2)}) collective-permute-start(bf16[256,256]{1,0:T(8,128)(2,1)S(1)} %all_gather.7), channel_id=1, source_target_pairs={{0,16},{8,24},{16,0},{24,8},{1,17},{9,25},{17,1},{25,9},{2,18},{10... | collective-permute-start | bytes 393224 | tf_op jit(solution)/shard_map/ppermute | solution.py:26
  420.0 10.6 %copy-start.10 = (pred[2048]{0:T(1024)(128)(4,1)S(1)}, pred[2048]{0:T(1024)(128)(4,1)}, u32[]{:S(2)}) copy-start(pred[2048]{0:T(1024)(128)(4,1)} %get-tuple-element.6) | copy-start | bytes 6148
Sparse Core Ops, SparseCore 0:
  206.8 137.6 reduce-scatter.1
where the time goes:
time: 442 us; the launch traced here: 441 us
  waiting for transfers between devices  140 us (32%)
  local copies, waits for them, and re-layouts  105 us (24%)
  other arithmetic  90.2 us (20%)
  blocking collectives  61.1 us (14%)
  matrix products  22.5 us (5%)
  between operations  14.3 us (3%)
  starting transfers between devices  7.18 us (2%)
    reduce_scatter x1, waiting for transfers between devices, body(): lax.psum_scatter(summed[:number], ('region', 'dom'), scatter_dimension=0,...  136 us
    scatter-add x1, other arithmetic, body(): jax.ops.segment_sum(message.astype(jnp.float32), edge_targets, num_segmen...  51.4 us
    gather x1, local copies, waits for them, and re-layouts, body(): jnp.take(from_side, edge_senders, axis=0).astype(jnp.float32)  36.9 us
    gather x1, local copies, waits for them, and re-layouts, body(): jnp.take(to_side, edge_targets, axis=0).astype(jnp.float32)  36.9 us
    all_gather x1, blocking collectives, body(): region_from = lax.all_gather(upper_from, 'dom', axis=0, tiled=True)  30.5 us
    all_gather x1, blocking collectives, body(): region_lifted = lax.all_gather(lifted, 'dom', axis=0, tiled=True)  30.5 us
    scatter-add x1, other arithmetic, body(): jax.ops.segment_sum(refined_wide, slot_ids, num_segments=number + 1)  12.2 us
    dot_general x1, matrix products, body(): jnp.dot(hidden, message_weight, preferred_element_type=jnp.float32)  12.1 us
  transfers between devices with their start and end apart: 4, of which 2 were waited for; matrix products, arithmetic and copies ran while one was open for 10% of the time, Pallas kernels for 0%

commit v1 on v0

v1 whole, which is shorter than its diff:
```python
import functools

import jax
import jax.numpy as jnp
from jax import lax
from jax.experimental import pallas as pl
from jax.experimental.pallas import tpu as pltpu
from jax.sharding import PartitionSpec as P

EDGE_TILE = 512
NODE_TILE = 512
F32 = jnp.float32
BF16 = jnp.bfloat16


def normalize(values):
    centered = values - jnp.mean(values, axis=-1, keepdims=True)
    variance = jnp.mean(centered * centered, axis=-1, keepdims=True)
    return centered * lax.rsqrt(variance + 1e-05)


def silu(values):
    return values * pl.reciprocal(1.0 + jnp.exp(-values), approx=False)


def mm(a, b):
    return jnp.dot(a, b, preferred_element_type=F32)


def hot_columns(row, width):
    count = row.shape[1]
    spread = jnp.transpose(jnp.broadcast_to(row, (128, count))).astype(jnp.int16)
    lane = lax.broadcasted_iota(jnp.int32, (count, 128), 1).astype(jnp.int16)
    one = jnp.ones((count, 128), BF16)
    zero = jnp.zeros((count, 128), BF16)
    return [
        jnp.where(spread == lane + jnp.int16(k * 128), one, zero) for k in range(width // 128)
    ]


def hot_rows(row, first, height):
    count = row.shape[1]
    spread = jnp.broadcast_to(row - first, (height, count)).astype(jnp.int16)
    place = lax.broadcasted_iota(jnp.int32, (height, count), 0).astype(jnp.int16)
    return jnp.where(spread == place, jnp.ones((height, count), BF16), jnp.zeros((height, count), BF16))


def fine_kernel(
    edge_steps,
    fine_ref,
    halo_ref,
    edges_ref,
    senders_ref,
    targets_ref,
    window_ref,
    sender_w,
    target_w,
    edge_w,
    message_w,
    self_w,
    inflow_w,
    update_w,
    refined_ref,
    pooled_ref,
    table,
    messages,
):
    step = pl.program_id(0)
    nodes = fine_ref.shape[0]
    extended = nodes + halo_ref.shape[0]
    tile = edges_ref.shape[0]

    @pl.when(step == 0)
    def _():
        table[:nodes] = mm(fine_ref[...], sender_w[...]).astype(BF16)
        table[nodes:extended] = mm(halo_ref[...], sender_w[...]).astype(BF16)
        table[extended : extended + nodes] = mm(fine_ref[...], target_w[...]).astype(BF16)
        table[extended + nodes :] = edge_w[...]
        pooled_ref[...] = jnp.zeros_like(pooled_ref)

    @pl.when(step < edge_steps)
    def _():
        s_row = senders_ref[pl.ds(step, 1)]
        t_row = targets_ref[pl.ds(step, 1)]
        pieces = hot_columns(s_row, extended) + hot_columns(t_row, nodes) + [edges_ref[...]]
        hidden = silu(mm(jnp.concatenate(pieces, axis=1), table[...])).astype(BF16)
        messages[pl.ds(pl.multiple_of(step * tile, tile), tile)] = normalize(
            mm(hidden, message_w[...])
        ).astype(BF16)

    @pl.when(step >= edge_steps)
    def _():
        number = step - edge_steps
        first = pl.multiple_of(number * NODE_TILE, NODE_TILE)
        here = pl.ds(first, NODE_TILE)
        hot = jnp.concatenate(
            [hot_rows(targets_ref[k : k + 1], first, NODE_TILE) for k in range(edge_steps)], axis=1
        )
        inflow = mm(hot, messages[...]).astype(BF16)
        own = fine_ref[here]
        node_hidden = silu(mm(own, self_w[...]) + mm(inflow, inflow_w[...])).astype(BF16)
        refined = (own.astype(F32) + normalize(mm(node_hidden, update_w[...]))).astype(BF16)
        refined_ref[here] = refined
        pooled_ref[...] += mm(hot_rows(window_ref[pl.ds(number, 1)], 0, pooled_ref.shape[0]), refined)


def fine_stage(fine, halo, edges, senders, targets, window_ids, window, weights):
    nodes, depth = fine.shape
    count = edges.shape[0]
    edge_steps = count // EDGE_TILE
    node_steps = nodes // NODE_TILE
    whole = pl.BlockSpec(memory_space=pltpu.VMEM)
    return pl.pallas_call(
        functools.partial(fine_kernel, edge_steps),
        grid=(edge_steps + node_steps,),
        out_shape=(
            jax.ShapeDtypeStruct((nodes, depth), BF16),
            jax.ShapeDtypeStruct((window, depth), F32),
        ),
        in_specs=[
            whole,
            whole,
            pl.BlockSpec((EDGE_TILE, depth), lambda i: (jnp.minimum(i, edge_steps - 1), 0)),
        ]
        + [whole] * 10,
        out_specs=(whole, whole),
        scratch_shapes=[
            pltpu.VMEM((2 * nodes + halo.shape[0] + depth, depth), BF16),
            pltpu.VMEM((count, depth), BF16),
        ],
        compiler_params=pltpu.CompilerParams(
            dimension_semantics=("arbitrary",), vmem_limit_bytes=56 * 2**20
        ),
        cost_estimate=pl.CostEstimate(
            flops=2 * depth * count * (3 * nodes + 3 * depth), bytes_accessed=8 * 2**20, transcendentals=0
        ),
    )(
        fine,
        halo,
        edges,
        senders.reshape(edge_steps, EDGE_TILE),
        targets.reshape(edge_steps, EDGE_TILE),
        window_ids.reshape(node_steps, NODE_TILE),
        *weights,
    )


def hot(ids, count):
    return (ids[:, None] == jnp.arange(count, dtype=ids.dtype)[None, :]).astype(BF16)


def body(
    fine_latents,
    edge_latents,
    send_rows,
    edge_senders,
    edge_targets,
    cluster_ids,
    coarse_latents,
    coarse_senders,
    coarse_targets,
    sender_weight,
    target_weight,
    edge_weight,
    message_weight,
    self_weight,
    inflow_weight,
    update_weight,
    pooling_weight,
    upper_sender,
    upper_target,
    upper_update,
    lifting_weight,
):
    halo_width = send_rows.shape[0] // 2
    region_index = lax.axis_index("region")
    dom_index = lax.axis_index("dom")
    dom_count = lax.axis_size("dom")
    region_count = lax.axis_size("region")
    owned = coarse_latents.shape[0]
    block = dom_count * owned
    exported = mm(hot(send_rows, fine_latents.shape[0]), fine_latents).astype(BF16)
    up = [(i, i + 1) for i in range(dom_count - 1)]
    down = [(i + 1, i) for i in range(dom_count - 1)]
    halo = jnp.concatenate(
        [
            lax.ppermute(exported[halo_width:], "dom", up),
            lax.ppermute(exported[:halo_width], "dom", down),
        ],
        axis=0,
    )
    is_partner = (cluster_ids // block != region_index).astype(jnp.int32)
    window_ids = cluster_ids % block + is_partner * block
    refined, partial = fine_stage(
        fine_latents,
        halo,
        edge_latents,
        edge_senders,
        edge_targets,
        window_ids,
        2 * block,
        (
            sender_weight,
            target_weight,
            edge_weight,
            message_weight,
            self_weight,
            inflow_weight,
            update_weight,
        ),
    )
    across = [(i, (i + region_count // 2) % region_count) for i in range(region_count)]
    summed = partial[:block] + lax.ppermute(partial[block:], "region", across)
    pooled = lax.psum_scatter(summed, "dom", scatter_dimension=0, tiled=True).astype(BF16)
    coarse_start = (coarse_latents.astype(F32) + mm(pooled, pooling_weight)).astype(BF16)
    upper_from = mm(coarse_start, upper_sender).astype(BF16)
    upper_to = mm(coarse_start, upper_target).astype(BF16)
    region_from = lax.all_gather(upper_from, "dom", axis=0, tiled=True)
    sender_slots = coarse_senders - region_index * block
    target_slots = coarse_targets - (region_index * dom_count + dom_index) * owned
    target_hot = hot(target_slots, owned)
    coarse_pre = mm(hot(sender_slots, block), region_from) + mm(target_hot, upper_to)
    coarse_message = jax.nn.silu(coarse_pre).astype(BF16)
    coarse_inflow = mm(target_hot.T, coarse_message).astype(BF16)
    coarse_update = normalize(mm(coarse_inflow, upper_update))
    coarse_out = (coarse_start.astype(F32) + coarse_update).astype(BF16)
    lifted = mm(coarse_out, lifting_weight).astype(BF16)
    region_lifted = lax.all_gather(lifted, "dom", axis=0, tiled=True)
    partner_lifted = lax.ppermute(region_lifted, "region", across)
    window_lifted = jnp.concatenate([region_lifted, partner_lifted], axis=0)
    fine_out = (refined.astype(F32) + mm(hot(window_ids, 2 * block), window_lifted)).astype(BF16)
    return (fine_out, coarse_out)


def solution(mesh):
    return jax.shard_map(
        body,
        mesh=mesh,
        in_specs=(
            P(("region", "dom"), None),
            P(("region", "dom"), None),
            P(("region", "dom")),
            P(("region", "dom")),
            P(("region", "dom")),
            P(("region", "dom")),
            P(("region", "dom"), None),
            P(("region", "dom")),
            P(("region", "dom")),
            P(),
            P(),
            P(),
            P(),
            P(),
            P(),
            P(),
            P(),
            P(),
            P(),
            P(),
            P(),
        ),
        out_specs=(P(("region", "dom"), None), P(("region", "dom"), None)),
        check_vma=False,
    )
```

time: 442 us -> 223 us (0.50)
  local copies, waits for them, and re-layouts: 105 us -> 2.89 us
  other arithmetic: 90.2 us -> 2.65 us
  waiting for transfers between devices: 140 us -> 74.1 us
  Pallas kernels: 0 us -> 52.6 us
  matrix products: 22.5 us -> 6.16 us
    gather x5 -> x0, local copies, waits for them, and re-layouts: 86.6 us -> none  [the longest x1 36.9 us: body(): jnp.take(from_side, edge_senders, axis=0).astype(jnp.float32)]
    reduce_scatter x1, waiting for transfers between devices: 136 us -> 62.5 us  [body(): lax.psum_scatter(summed, 'dom', scatter_dimension=0, tiled=True)]
    scatter-add x3 -> x0, other arithmetic: 70.1 us -> none  [the longest x1 51.4 us: body(): jax.ops.segment_sum(message.astype(jnp.float32), edge_targets, num_segmen...]
    pallas_call x0 -> x1, Pallas kernels: none -> 52.6 us  [fine_stage(): pl.pallas_call(functools.partial(fine_kernel, edge_steps), grid=(edge_ste...]
    dot_general x10 -> x8, matrix products: 22.5 us -> 6.16 us  [mm(): return jnp.dot(a, b, preferred_element_type=F32)]
    convert_element_type x2 -> x0, local copies, waits for them, and re-layouts: 11.5 us -> none  [the longest x1 9.66 us: body(): message.astype(jnp.float32)]
    convert_element_type x4 -> x1, other arithmetic: 8.13 us -> 0.08 us  [body(): coarse_out = (coarse_start.astype(F32) + coarse_update).astype(BF16)]
    ppermute x3 -> x4, waiting for transfers between devices: 4.59 us -> 11.6 us  [the longest x1 5.13 us: body(): summed = partial[:block] + lax.ppermute(partial[block:], 'region', across)]
  transfers between devices with their start and end apart: 4 -> 5, of which waited for: 2 -> 4; matrix products, arithmetic and copies ran while one was open for 10% -> 1% of each run, Pallas kernels for 0% -> 0%
where the time goes in v1:
time: 223 us
  waiting for transfers between devices  74.1 us (33%)
  blocking collectives  61.3 us (27%)
  Pallas kernels  52.6 us (24%)
  between operations  14.2 us (6%)
  starting transfers between devices  9.18 us (4%)
  matrix products  6.16 us (3%)
  local copies, waits for them, and re-layouts  2.89 us (1%)
  other arithmetic  2.65 us (1%)
    reduce_scatter x1, waiting for transfers between devices, body(): lax.psum_scatter(summed, 'dom', scatter_dimension=0, tiled=True)  62.5 us
    pallas_call x1, Pallas kernels, fine_stage(): pl.pallas_call(functools.partial(fine_kernel, edge_steps), grid=(edge_ste...  52.6 us
    all_gather x1, blocking collectives, body(): region_from = lax.all_gather(upper_from, 'dom', axis=0, tiled=True)  30.7 us
    all_gather x1, blocking collectives, body(): region_lifted = lax.all_gather(lifted, 'dom', axis=0, tiled=True)  30.5 us
    dot_general x8, matrix products, mm(): return jnp.dot(a, b, preferred_element_type=F32)  6.16 us
    ppermute x1, waiting for transfers between devices, body(): summed = partial[:block] + lax.ppermute(partial[block:], 'region', across)  5.13 us
    ppermute x1, starting transfers between devices, body(): lax.ppermute(exported[halo_width:], 'dom', up)  4.87 us
  transfers between devices with their start and end apart: 5, of which 4 were waited for; matrix products, arithmetic and copies ran while one was open for 1% of the time, Pallas kernels for 0%

profile of v1, /device:TPU:0, one launch (start us, length us, event | category | flops | bytes accessed | tf_op | source)
XLA Modules:
  0.0 223.1 jit_solution(15905043539377063404)
XLA Ops:
  7.3 1.8 fusion.3
  9.0 4.9 %collective-permute-start = (bf16[128,256]{1,0:T(8,128)(2,1)S(1)}, bf16[128,256]{1,0:T(8,128)(2,1)S(1)}, u32[]{:S(2)}, u32[]{:S(2)}) collective-permute-start(bf16[128,256]{1,0:T(8,128)(2,1)S(1)} %get-tuple-element.6), channel_id=1, source_target_pairs={{0,1},{1,2},{2,3},{3,4},{4,5},{5,6},{6,7},{8,9},{9,10},{10,11},{11... | collective-permute-start | bytes 196616 | tf_op jit(solution)/shard_map/ppermute | solution.py:187
  13.9 1.3 collective-permute-start.1
  15.3 0.6 reshape.31.window_ref
  15.9 0.6 reshape.29.senders_ref
  16.5 0.6 reshape.30.targets_ref
  17.1 3.0 %collective-permute-done.1 = bf16[128,256]{1,0:T(8,128)(2,1)S(1)} collective-permute-done((bf16[128,256]{1,0:T(8,128)(2,1)S(1)}, bf16[128,256]{1,0:T(8,128)(2,1)S(1)}, u32[]{:S(2)}, u32[]{:S(2)}) %collective-permute-start.1) | collective-permute-done | bytes 65568 | tf_op jit(solution)/shard_map/ppermute | solution.py:188
  20.1 0.7 pad_maximum_fusion.halo_ref
  20.8 52.6 %shard_map.212 = (bf16[2048,256]{1,0:T(8,128)(2,1)}, f32[512,256]{1,0:T(8,128)}) custom-call(bf16[2048,256]{1,0:T(8,128)(2,1)} %fine_ref.1, bf16[256,256]{1,0:T(8,128)(2,1)} %pad_maximum_fusion.halo_ref, bf16[9216,256]{1,0:T(8,128)(2,1)} %edges_ref.1, s32[18,512]{1,0:T(8,128)} %reshape.29.senders_ref, s32[18,512]{1,0:T(8,128)} %reshape.30.targets_ref, ...), custom_call_target="tpu_custom_call" | custom-call | flops 32614907904 | bytes 8388608 | tf_op jit(solution)/shard_map/pallas_call | solution.py:113
  73.4 1.0 slice.15
  74.4 1.6 collective-permute-start.2
  75.9 5.1 %collective-permute-done.2 = f32[256,256]{1,0:T(8,128)S(1)} collective-permute-done((f32[256,256]{1,0:T(8,128)S(1)}, f32[256,256]{1,0:T(8,128)S(1)}, u32[]{:S(2)}, u32[]{:S(2)}) %collective-permute-start.2) | collective-permute-done | bytes 262176 | tf_op jit(solution)/shard_map/ppermute | solution.py:213
  81.0 1.7 slice_add_fusion
  82.8 62.5 %reduce-scatter.2.cloned.1.call-done = f32[32,256]{1,0:T(8,128)} async-done(((f32[256,256]{1,0:T(8,128)}), f32[32,256]{1,0:T(8,128)}) %reduce-scatter.2.cloned.1.call-update) | async-done | bytes 32784 | tf_op jit(solution)/shard_map/reduce_scatter | solution.py:214
  145.3 0.9 fusion.4
  146.3 30.7 %all_gather.6 = bf16[256,256]{1,0:T(8,128)(2,1)S(1)} all-gather(bf16[32,256]{1,0:T(8,128)(2,1)S(1)} %convolution_convert_fusion.3), channel_id=1, replica_groups=mesh['region'=4,'dom'=8] {'dom'}, dimensions={0}, use_global_device_ids=true | all-gather | bytes 147456 | tf_op jit(solution)/shard_map/all_gather | solution.py:218
  177.1 0.3 fusion.7
  177.4 0.4 multiply_convert_fusion
  177.8 0.5 fusion.24
  178.4 0.2 multiply_reduce_fusion
  178.8 30.5 %all_gather.7 = bf16[256,256]{1,0:T(8,128)(2,1)S(1)} all-gather(bf16[32,256]{1,0:T(8,128)(2,1)S(1)} %convolution_convert_fusion), channel_id=1, replica_groups=mesh['region'=4,'dom'=8] {'dom'}, dimensions={0}, use_global_device_ids=true | all-gather | bytes 147456 | tf_op jit(solution)/shard_map/all_gather | solution.py:228
  209.3 1.4 collective-permute-start.3
  210.8 3.5 %collective-permute-done.3 = bf16[256,256]{1,0:T(8,128)(2,1)S(1)} collective-permute-done((bf16[256,256]{1,0:T(8,128)(2,1)S(1)}, bf16[256,256]{1,0:T(8,128)(2,1)S(1)}, u32[]{:S(2)}, u32[]{:S(2)}) %collective-permute-start.3) | collective-permute-done | bytes 131104 | tf_op jit(solution)/shard_map/ppermute | solution.py:229
  214.3 2.0 add_convert_fusion
  (38 shorter events, 0.5 us)
Async XLA Ops:
  7.2 170.2 %copy-start = (bf16[256,256]{1,0:T(8,128)(2,1)S(1)}, bf16[256,256]{1,0:T(8,128)(2,1)}, u32[]{:S(2)}) copy-start(bf16[256,256]{1,0:T(8,128)(2,1)} %param.39) | copy-start | bytes 393220
  7.2 8.0 %copy-start.9 = (s32[2048]{0:T(1024)S(1)}, s32[2048]{0:T(1024)}, u32[]{:S(2)}) copy-start(s32[2048]{0:T(1024)} %param.26) | copy-start | bytes 24580
  7.2 8.7 %copy-start.6 = (s32[9216]{0:T(1024)S(1)}, s32[9216]{0:T(1024)}, u32[]{:S(2)}) copy-start(s32[9216]{0:T(1024)} %param.24) | copy-start | bytes 110596
  7.2 9.3 %copy-start.7 = (s32[9216]{0:T(1024)S(1)}, s32[9216]{0:T(1024)}, u32[]{:S(2)}) copy-start(s32[9216]{0:T(1024)} %param.25) | copy-start | bytes 110596
  7.2 138.1 %reduce-scatter.2.cloned.1.call-start = ((), (), s32[]{:S(2)}) async-start(), calls=%async_computation.1 | async-start | bytes 294912 | tf_op jit(solution)/shard_map/reduce_scatter | solution.py:214
  9.0 8.1 %collective-permute-start = (bf16[128,256]{1,0:T(8,128)(2,1)S(1)}, bf16[128,256]{1,0:T(8,128)(2,1)S(1)}, u32[]{:S(2)}, u32[]{:S(2)}) collective-permute-start(bf16[128,256]{1,0:T(8,128)(2,1)S(1)} %get-tuple-element.6), channel_id=1, source_target_pairs={{0,1},{1,2},{2,3},{3,4},{4,5},{5,6},{6,7},{8,9},{9,10},{10,11},{11... | collective-permute-start | bytes 196616 | tf_op jit(solution)/shard_map/ppermute | solution.py:187
  13.9 6.2 %collective-permute-start.1 = (bf16[128,256]{1,0:T(8,128)(2,1)S(1)}, bf16[128,256]{1,0:T(8,128)(2,1)S(1)}, u32[]{:S(2)}, u32[]{:S(2)}) collective-permute-start(bf16[128,256]{1,0:T(8,128)(2,1)S(1)} %get-tuple-element.7), channel_id=1, source_target_pairs={{1,0},{2,1},{3,2},{4,3},{5,4},{6,5},{7,6},{9,8},{10,9},{11,10},{12... | collective-permute-start | bytes 196616 | tf_op jit(solution)/shard_map/ppermute | solution.py:188
  20.7 62.0 %copy-start.10 = (s32[512]{0:T(512)S(1)}, s32[512]{0:T(512)}, u32[]{:S(2)}) copy-start(s32[512]{0:T(512)} %param.29) | copy-start | bytes 6148
  20.7 62.1 %copy-start.11 = (s32[512]{0:T(512)S(1)}, s32[512]{0:T(512)}, u32[]{:S(2)}) copy-start(s32[512]{0:T(512)} %param.28) | copy-start | bytes 6148
  20.7 124.5 %copy-start.3 = (bf16[256,256]{1,0:T(8,128)(2,1)S(1)}, bf16[256,256]{1,0:T(8,128)(2,1)}, u32[]{:S(2)}) copy-start(bf16[256,256]{1,0:T(8,128)(2,1)} %param.37) | copy-start | bytes 393220
  20.7 124.5 %copy-start.8 = (bf16[32,256]{1,0:T(8,128)(2,1)S(1)}, bf16[32,256]{1,0:T(8,128)(2,1)}, u32[]{:S(2)}) copy-start(bf16[32,256]{1,0:T(8,128)(2,1)} %param.27) | copy-start | bytes 49156
  20.8 125.4 %copy-start.1 = (bf16[256,256]{1,0:T(8,128)(2,1)S(1)}, bf16[256,256]{1,0:T(8,128)(2,1)}, u32[]{:S(2)}) copy-start(bf16[256,256]{1,0:T(8,128)(2,1)} %param.38) | copy-start | bytes 393220
  74.4 6.7 %collective-permute-start.2 = (f32[256,256]{1,0:T(8,128)S(1)}, f32[256,256]{1,0:T(8,128)S(1)}, u32[]{:S(2)}, u32[]{:S(2)}) collective-permute-start(f32[256,256]{1,0:T(8,128)S(1)} %slice.15), channel_id=1, source_target_pairs={{0,16},{8,24},{16,0},{24,8},{1,17},{9,25},{17,1},{25,9},{2,18},{10... | collective-permute-start | bytes 786440 | tf_op jit(solution)/shard_map/ppermute | solution.py:213
  82.7 95.1 %copy-start.4 = (bf16[256,256]{1,0:T(8,128)(2,1)S(1)}, bf16[256,256]{1,0:T(8,128)(2,1)}, u32[]{:S(2)}) copy-start(bf16[256,256]{1,0:T(8,128)(2,1)} %param.40) | copy-start | bytes 393220
  82.8 95.8 %copy-start.2 = (bf16[256,256]{1,0:T(8,128)(2,1)S(1)}, bf16[256,256]{1,0:T(8,128)(2,1)}, u32[]{:S(2)}) copy-start(bf16[256,256]{1,0:T(8,128)(2,1)} %param.41) | copy-start | bytes 393220
  146.3 68.0 %copy-start.12 = (bf16[2048,256]{1,0:T(8,128)(2,1)S(1)}, bf16[2048,256]{1,0:T(8,128)(2,1)}, u32[]{:S(2)}) copy-start(bf16[2048,256]{1,0:T(8,128)(2,1)} %get-tuple-element.4) | copy-start | bytes 3145732
  178.7 37.6 %copy-start.5 = (bf16[32,256]{1,0:T(8,128)(2,1)}, bf16[32,256]{1,0:T(8,128)(2,1)S(1)}, u32[]{:S(2)}) copy-start(bf16[32,256]{1,0:T(8,128)(2,1)S(1)} %add_convert_fusion.1) | copy-start | bytes 49156
  209.3 5.0 %collective-permute-start.3 = (bf16[256,256]{1,0:T(8,128)(2,1)S(1)}, bf16[256,256]{1,0:T(8,128)(2,1)S(1)}, u32[]{:S(2)}, u32[]{:S(2)}) collective-permute-start(bf16[256,256]{1,0:T(8,128)(2,1)S(1)} %all_gather.7), channel_id=1, source_target_pairs={{0,16},{8,24},{16,0},{24,8},{1,17},{9,25},{17,1},{25,9},{2,18},{10... | collective-permute-start | bytes 393224 | tf_op jit(solution)/shard_map/ppermute | solution.py:229
Sparse Core Ops, SparseCore 0:
  82.9 62.3 reduce-scatter.1

commit v2 on v1

--- a/solution.py
+++ b/solution.py
@@ -64,6 +64,7 @@
     pooled_ref,
     table,
     messages,
+    pooled,
 ):
     step = pl.program_id(0)
     nodes = fine_ref.shape[0]
@@ -76,7 +77,7 @@
         table[nodes:extended] = mm(halo_ref[...], sender_w[...]).astype(BF16)
         table[extended : extended + nodes] = mm(fine_ref[...], target_w[...]).astype(BF16)
         table[extended + nodes :] = edge_w[...]
-        pooled_ref[...] = jnp.zeros_like(pooled_ref)
+        pooled[...] = jnp.zeros_like(pooled)
 
     @pl.when(step < edge_steps)
     def _():
@@ -101,7 +102,11 @@
         node_hidden = silu(mm(own, self_w[...]) + mm(inflow, inflow_w[...])).astype(BF16)
         refined = (own.astype(F32) + normalize(mm(node_hidden, update_w[...]))).astype(BF16)
         refined_ref[here] = refined
-        pooled_ref[...] += mm(hot_rows(window_ref[pl.ds(number, 1)], 0, pooled_ref.shape[0]), refined)
+        pooled[...] += mm(hot_rows(window_ref[pl.ds(number, 1)], 0, pooled.shape[0]), refined)
+
+    @pl.when(step == pl.num_programs(0) - 1)
+    def _():
+        pooled_ref[...] = pooled[...].astype(BF16)
 
 
 def fine_stage(fine, halo, edges, senders, targets, window_ids, window, weights):
@@ -115,7 +120,7 @@
         grid=(edge_steps + node_steps,),
         out_shape=(
             jax.ShapeDtypeStruct((nodes, depth), BF16),
-            jax.ShapeDtypeStruct((window, depth), F32),
+            jax.ShapeDtypeStruct((window, depth), BF16),
         ),
         in_specs=[
             whole,
@@ -127,6 +132,7 @@
         scratch_shapes=[
             pltpu.VMEM((2 * nodes + halo.shape[0] + depth, depth), BF16),
             pltpu.VMEM((count, depth), BF16),
+            pltpu.VMEM((window, depth), F32),
         ],
         compiler_params=pltpu.CompilerParams(
             dimension_semantics=("arbitrary",), vmem_limit_bytes=56 * 2**20
@@ -145,8 +151,239 @@
     )
 
 
-def hot(ids, count):
-    return (ids[:, None] == jnp.arange(count, dtype=ids.dtype)[None, :]).astype(BF16)
+def to_device(src, dst, sends, receives, slot, region, dom):
+    return pltpu.make_async_remote_copy(
+        src_ref=src,
+        dst_ref=dst,
+        send_sem=sends.at[slot],
+        recv_sem=receives.at[slot],
+        device_id=(region, dom),
+        device_id_type=pl.DeviceIdType.MESH,
+    )
+
+
+def halo_kernel(doms, fine_ref, rows_ref, halo_ref, exported, landed, sends, receives):
+    region, me = lax.axis_index("region"), lax.axis_index("dom")
+    above, below = lax.rem(me + 1, doms), lax.rem(me + doms - 1, doms)
+    barrier = pltpu.get_barrier_semaphore()
+    for other in (above, below):
+        pl.semaphore_signal(
+            barrier, inc=1, device_id=(region, other), device_id_type=pl.DeviceIdType.MESH
+        )
+    width = rows_ref.shape[1] // 2
+    hot = jnp.concatenate(hot_columns(rows_ref[...], fine_ref.shape[0]), axis=1)
+    exported[...] = mm(hot, fine_ref[...]).astype(BF16)
+    pl.semaphore_wait(barrier, 2)
+    lower, upper = pl.ds(0, width), pl.ds(width, width)
+    copies = [
+        to_device(exported.at[upper], landed.at[lower], sends, receives, 0, region, above),
+        to_device(exported.at[lower], landed.at[upper], sends, receives, 1, region, below),
+    ]
+    for copy in copies:
+        copy.start()
+    for copy in copies:
+        copy.wait()
+    zeros = jnp.zeros((width, fine_ref.shape[1]), BF16)
+    halo_ref[lower] = jnp.where(me > 0, landed[lower], zeros)
+    halo_ref[upper] = jnp.where(me < doms - 1, landed[upper], zeros)
+
+
+def halo_stage(fine, send_rows, doms):
+    whole = pl.BlockSpec(memory_space=pltpu.VMEM)
+    shape = (send_rows.shape[0], fine.shape[1])
+    return pl.pallas_call(
+        functools.partial(halo_kernel, doms),
+        out_shape=jax.ShapeDtypeStruct(shape, BF16),
+        in_specs=[whole] * 2,
+        out_specs=whole,
+        scratch_shapes=[
+            pltpu.VMEM(shape, BF16),
+            pltpu.VMEM(shape, BF16),
+            pltpu.SemaphoreType.DMA((2,)),
+            pltpu.SemaphoreType.DMA((2,)),
+        ],
+        compiler_params=pltpu.CompilerParams(
+            collective_id=0, has_side_effects=True, vmem_limit_bytes=32 * 2**20
+        ),
+    )(fine, send_rows.reshape(1, -1))
+
+
+def coarse_kernel(
+    regions,
+    doms,
+    partial_ref,
+    refined_ref,
+    latents_ref,
+    senders_ref,
+    targets_ref,
+    window_ref,
+    pooling_w,
+    sender_w,
+    target_w,
+    update_w,
+    lifting_w,
+    fine_ref,
+    coarse_ref,
+    arrived,
+    region_from,
+    lifted,
+    chosen,
+    picked,
+    pool_send,
+    pool_recv,
+    from_send,
+    from_recv,
+    lift_send,
+    lift_recv,
+):
+    region, me = lax.axis_index("region"), lax.axis_index("dom")
+    partner = lax.rem(region + regions // 2, regions)
+    owned = latents_ref.shape[0]
+    block = doms * owned
+
+    def part(dom, base=0):
+        return pl.ds(base + pl.multiple_of(dom * owned, owned), owned)
+
+    peers = [lax.rem(me + k, doms) for k in range(doms)]
+    barrier = pltpu.get_barrier_semaphore()
+    for k in range(doms):
+        if k:
+            pl.semaphore_signal(
+                barrier, inc=1, device_id=(region, peers[k]), device_id_type=pl.DeviceIdType.MESH
+            )
+        pl.semaphore_signal(
+            barrier, inc=1, device_id=(partner, peers[k]), device_id_type=pl.DeviceIdType.MESH
+        )
+    pl.semaphore_wait(barrier, 2 * doms - 1)
+
+    pool = []
+    for k in range(doms):
+        pool.append(
+            to_device(
+                partial_ref.at[part(peers[k], block)],
+                arrived.at[doms + k],
+                pool_send,
+                pool_recv,
+                doms + k,
+                partner,
+                peers[k],
+            )
+        )
+        if k:
+            pool.append(
+                to_device(
+                    partial_ref.at[part(peers[k])],
+                    arrived.at[k],
+                    pool_send,
+                    pool_recv,
+                    k,
+                    region,
+                    peers[k],
+                )
+            )
+    for copy in pool:
+        copy.start()
+    picked[...] = jnp.concatenate(hot_columns(senders_ref[...], block), axis=1)
+    for n in range(window_ref.shape[0]):
+        chosen[pl.ds(n * NODE_TILE, NODE_TILE)] = jnp.concatenate(
+            hot_columns(window_ref[n : n + 1], 2 * block), axis=1
+        )
+    target_row = hot_rows(targets_ref[...], 0, owned)
+    total = partial_ref[part(me)].astype(F32)
+    for copy in pool:
+        copy.wait_recv()
+    for k in range(1, 2 * doms):
+        total = total + arrived[k].astype(F32)
+    start = (latents_ref[...].astype(F32) + mm(total.astype(BF16), pooling_w[...])).astype(BF16)
+    region_from[part(me)] = mm(start, sender_w[...]).astype(BF16)
+    shares = [
+        to_device(
+            region_from.at[part(me)], region_from.at[part(me)], from_send, from_recv, k, region, peers[k]
+        )
+        for k in range(1, doms)
+    ]
+    for copy in shares:
+        copy.start()
+    upper_to = mm(start, target_w[...]).astype(BF16)
+    to_rows = lax.dot_general(
+        target_row, upper_to, (((0,), (0,)), ((), ())), preferred_element_type=F32
+    )
+    for copy in shares:
+        copy.wait_recv()
+    message = silu(mm(picked[...], region_from[...]) + to_rows).astype(BF16)
+    inflow = mm(target_row, message).astype(BF16)
+    result = (start.astype(F32) + normalize(mm(inflow, update_w[...]))).astype(BF16)
+    coarse_ref[...] = result
+    lifted[part(me)] = mm(result, lifting_w[...]).astype(BF16)
+    lifts = []
+    for k in range(doms):
+        lifts.append(
+            to_device(
+                lifted.at[part(me)],
+                lifted.at[part(me, block)],
+                lift_send,
+                lift_recv,
+                doms + k,
+                partner,
+                peers[k],
+            )
+        )
+        if k:
+            lifts.append(
+                to_device(
+                    lifted.at[part(me)], lifted.at[part(me)], lift_send, lift_recv, k, region, peers[k]
+                )
+            )
+    for copy in lifts:
+        copy.start()
+    for copy in pool + shares:
+        copy.wait_send()
+    for copy in lifts:
+        copy.wait_recv()
+    for n in range(window_ref.shape[0]):
+        rows = pl.ds(n * NODE_TILE, NODE_TILE)
+        fine_ref[rows] = (
+            refined_ref[rows].astype(F32) + mm(chosen[rows], lifted[...])
+        ).astype(BF16)
+    for copy in lifts:
+        copy.wait_send()
+
+
+def coarse_stage(partial, refined, latents, senders, targets, window_ids, weights, regions, doms):
+    whole = pl.BlockSpec(memory_space=pltpu.VMEM)
+    nodes, depth = refined.shape
+    owned = latents.shape[0]
+    block = doms * owned
+    count = senders.shape[0]
+    pair = [pltpu.SemaphoreType.DMA((2 * doms,))] * 2
+    return pl.pallas_call(
+        functools.partial(coarse_kernel, regions, doms),
+        out_shape=(
+            jax.ShapeDtypeStruct((nodes, depth), BF16),
+            jax.ShapeDtypeStruct((owned, depth), BF16),
+        ),
+        in_specs=[whole] * 11,
+        out_specs=(whole, whole),
+        scratch_shapes=[
+            pltpu.VMEM((2 * doms, owned, depth), BF16),
+            pltpu.VMEM((block, depth), BF16),
+            pltpu.VMEM((2 * block, depth), BF16),
+            pltpu.VMEM((nodes, 2 * block), BF16),
+            pltpu.VMEM((count, block), BF16),
+        ]
+        + pair * 3,
+        compiler_params=pltpu.CompilerParams(
+            collective_id=1, has_side_effects=True, vmem_limit_bytes=48 * 2**20
+        ),
+    )(
+        partial,
+        refined,
+        latents,
+        senders.reshape(1, -1),
+        targets.reshape(1, -1),
+        window_ids.reshape(-1, NODE_TILE),
+        *weights,
+    )
 
 
 def body(
@@ -172,23 +409,13 @@
     upper_update,
     lifting_weight,
 ):
-    halo_width = send_rows.shape[0] // 2
     region_index = lax.axis_index("region")
     dom_index = lax.axis_index("dom")
     dom_count = lax.axis_size("dom")
     region_count = lax.axis_size("region")
     owned = coarse_latents.shape[0]
     block = dom_count * owned
-    exported = mm(hot(send_rows, fine_latents.shape[0]), fine_latents).astype(BF16)
-    up = [(i, i + 1) for i in range(dom_count - 1)]
-    down = [(i + 1, i) for i in range(dom_count - 1)]
-    halo = jnp.concatenate(
-        [
-            lax.ppermute(exported[halo_width:], "dom", up),
-            lax.ppermute(exported[:halo_width], "dom", down),
-        ],
-        axis=0,
-    )
+    halo = halo_stage(fine_latents, send_rows, dom_count)
     is_partner = (cluster_ids // block != region_index).astype(jnp.int32)
     window_ids = cluster_ids % block + is_partner * block
     refined, partial = fine_stage(
@@ -209,26 +436,17 @@
             update_weight,
         ),
     )
-    across = [(i, (i + region_count // 2) % region_count) for i in range(region_count)]
-    summed = partial[:block] + lax.ppermute(partial[block:], "region", across)
-    pooled = lax.psum_scatter(summed, "dom", scatter_dimension=0, tiled=True).astype(BF16)
-    coarse_start = (coarse_latents.astype(F32) + mm(pooled, pooling_weight)).astype(BF16)
-    upper_from = mm(coarse_start, upper_sender).astype(BF16)
-    upper_to = mm(coarse_start, upper_target).astype(BF16)
-    region_from = lax.all_gather(upper_from, "dom", axis=0, tiled=True)
-    sender_slots = coarse_senders - region_index * block
-    target_slots = coarse_targets - (region_index * dom_count + dom_index) * owned
-    target_hot = hot(target_slots, owned)
-    coarse_pre = mm(hot(sender_slots, block), region_from) + mm(target_hot, upper_to)
-    coarse_message = jax.nn.silu(coarse_pre).astype(BF16)
-    coarse_inflow = mm(target_hot.T, coarse_message).astype(BF16)
-    coarse_update = normalize(mm(coarse_inflow, upper_update))
-    coarse_out = (coarse_start.astype(F32) + coarse_update).astype(BF16)
-    lifted = mm(coarse_out, lifting_weight).astype(BF16)
-    region_lifted = lax.all_gather(lifted, "dom", axis=0, tiled=True)
-    partner_lifted = lax.ppermute(region_lifted, "region", across)
-    window_lifted = jnp.concatenate([region_lifted, partner_lifted], axis=0)
-    fine_out = (refined.astype(F32) + mm(hot(window_ids, 2 * block), window_lifted)).astype(BF16)
+    fine_out, coarse_out = coarse_stage(
+        partial,
+        refined,
+        coarse_latents,
+        coarse_senders - region_index * block,
+        coarse_targets - (region_index * dom_count + dom_index) * owned,
+        window_ids,
+        (pooling_weight, upper_sender, upper_target, upper_update, lifting_weight),
+        region_count,
+        dom_count,
+    )
     return (fine_out, coarse_out)
 
 

time: 223 us -> 99.8 us (0.45)
  waiting for transfers between devices: 74.1 us -> 0 us
  blocking collectives: 61.3 us -> 0 us
  Pallas kernels: 52.6 us -> 86.8 us
  between operations: 14.2 us -> 0.75 us
  starting transfers between devices: 9.18 us -> 0 us
  local copies, waits for them, and re-layouts: 2.89 us -> 9.71 us
  matrix products: 6.16 us -> 0 us
    reduce_scatter x1 -> x0, waiting for transfers between devices: 62.5 us -> none  [body(): lax.psum_scatter(summed, 'dom', scatter_dimension=0, tiled=True)]
    all_gather x2 -> x0, blocking collectives: 61.3 us -> none  [the longest x1 30.7 us: body(): region_from = lax.all_gather(upper_from, 'dom', axis=0, tiled=True)]
    pallas_call x0 -> x2, Pallas kernels: none -> 34.1 us  [the longest x1 25.3 us: coarse_stage(): pl.pallas_call(functools.partial(coarse_kernel, regions, doms), out_shape...]
    ppermute x4 -> x0, waiting for transfers between devices: 11.6 us -> none  [the longest x1 5.13 us: body(): summed = partial[:block] + lax.ppermute(partial[block:], 'region', across)]
    ppermute x4 -> x0, starting transfers between devices: 9.14 us -> none  [the longest x1 4.87 us: body(): lax.ppermute(exported[halo_width:], 'dom', up)]
    unnamed x26, local copies, waits for them, and re-layouts: 0.07 us -> 6.33 us
    dot_general x8 -> x0, matrix products: 6.16 us -> none  [mm(): return jnp.dot(a, b, preferred_element_type=F32)]
  transfers between devices with their start and end apart: 5 -> 0, of which waited for: 4 -> 0; matrix products, arithmetic and copies ran while one was open for 1% -> 0% of each run, Pallas kernels for 0% -> 0%
where the time goes in v2:
time: 99.8 us; the launch traced here: 99.3 us
  Pallas kernels  86.8 us (87%)
  local copies, waits for them, and re-layouts  9.71 us (10%)
  other arithmetic  2.08 us (2%)
    pallas_call x1, Pallas kernels, fine_stage(): pl.pallas_call(functools.partial(fine_kernel, edge_steps), grid=(edge_ste...  52.6 us
    pallas_call x1, Pallas kernels, coarse_stage(): pl.pallas_call(functools.partial(coarse_kernel, regions, doms), out_shape...  25.3 us
    pallas_call x1, Pallas kernels, halo_stage(): pl.pallas_call(functools.partial(halo_kernel, doms), out_shape=jax.ShapeD...  8.8 us
    unnamed x26, local copies, waits for them, and re-layouts  6.33 us

profile of v2, /device:TPU:0, one launch (start us, length us, event | category | flops | bytes accessed | tf_op | source)
XLA Modules:
  0.0 99.3 jit_solution(10166997074803716821)
XLA Ops:
  0.6 0.7 broadcast_subtract_fusion.1
  1.3 0.7 broadcast_subtract_fusion
  2.0 0.7 fusion
  2.7 0.6 reshape.26.window_ref
  3.3 1.4 %reshape.24.senders_ref = s32[18,512]{1,0:T(8,128)} reshape(s32[9216]{0:T(1024)} %param.24) | data formatting | bytes 73728 | tf_op jit(solution)/shard_map/reshape | solution.py:147
  4.7 1.4 %reshape.25.targets_ref = s32[18,512]{1,0:T(8,128)} reshape(s32[9216]{0:T(1024)} %param.25) | data formatting | bytes 73728 | tf_op jit(solution)/shard_map/reshape | solution.py:148
  6.1 1.2 %copy-done = bf16[2048,256]{1,0:T(8,128)(2,1)S(1)} copy-done((bf16[2048,256]{1,0:T(8,128)(2,1)S(1)}, bf16[2048,256]{1,0:T(8,128)(2,1)}, u32[]{:S(2)}) %copy-start) | copy-done | bytes 1048600
  7.3 0.7 copy-done.11
  8.0 8.8 %shard_map.212.halo_ref = bf16[256,256]{1,0:T(8,128)(2,1)S(1)} custom-call(bf16[2048,256]{1,0:T(8,128)(2,1)S(1)} %copy-done, s32[1,256]{1,0:T(1,128)S(1)} %bitcast.5), custom_call_target="tpu_custom_call" | custom-call | tf_op jit(solution)/shard_map/pallas_call | solution.py:194
  16.8 0.0 copy-start.3
  16.8 0.6 copy-done.3
  17.5 0.0 copy-start.8
  17.5 0.0 copy-start.9
  17.5 0.0 copy-start.10
  17.5 52.6 %shard_map.213 = (bf16[2048,256]{1,0:T(8,128)(2,1)}, bf16[512,256]{1,0:T(8,128)(2,1)}) custom-call(bf16[2048,256]{1,0:T(8,128)(2,1)} %fine_ref.3, bf16[256,256]{1,0:T(8,128)(2,1)} %copy-done.3, bf16[9216,256]{1,0:T(8,128)(2,1)} %edges_ref.1, s32[18,512]{1,0:T(8,128)} %reshape.24.senders_ref, s32[18,512]{1,0:T(8,128)} %reshape.25.targets_ref, ...), custom_call_target="tpu_custom_call" | custom-call | flops 32614907904 | bytes 8388608 | tf_op jit(solution)/shard_map/pallas_call | solution.py:118
  70.1 0.0 copy-done.4
  70.1 0.0 copy-done.5
  70.1 0.0 copy-done.6
  70.2 0.0 copy-start.1
  70.2 1.2 %copy-done.1 = bf16[2048,256]{1,0:T(8,128)(2,1)S(1)} copy-done((bf16[2048,256]{1,0:T(8,128)(2,1)S(1)}, bf16[2048,256]{1,0:T(8,128)(2,1)}, u32[]{:S(2)}) %copy-start.1) | copy-done | bytes 1048600
  71.4 0.9 copy-done.2
  72.4 25.3 %shard_map.214 = (bf16[2048,256]{1,0:T(8,128)(2,1)S(1)}, bf16[32,256]{1,0:T(8,128)(2,1)S(1)}) custom-call(bf16[512,256]{1,0:T(8,128)(2,1)S(1)} %copy-done.2, bf16[2048,256]{1,0:T(8,128)(2,1)S(1)} %copy-done.1, bf16[32,256]{1,0:T(8,128)(2,1)S(1)} %copy-done.10, s32[1,512]{1,0:T(1,128)S(1)} %bitcast.3, s32[1,512]{1,0:T(1,128)S(1)} %bitcast.4, ...), custom_call_target="tpu_custom_call" | custom-call | tf_op jit(solution)/shard_map/pallas_call | solution.py:359
  97.7 1.0 copy.25
  98.7 0.6 copy.26
  (11 shorter events, 0.0 us)
Async XLA Ops:
  6.1 1.2 %copy-start = (bf16[2048,256]{1,0:T(8,128)(2,1)S(1)}, bf16[2048,256]{1,0:T(8,128)(2,1)}, u32[]{:S(2)}) copy-start(bf16[2048,256]{1,0:T(8,128)(2,1)} %fine_ref.3) | copy-start | bytes 3145732
  7.3 0.7 copy-start.11
  16.8 0.7 copy-start.3
  17.5 52.7 %copy-start.4 = (bf16[256,256]{1,0:T(8,128)(2,1)S(1)}, bf16[256,256]{1,0:T(8,128)(2,1)}, u32[]{:S(2)}) copy-start(bf16[256,256]{1,0:T(8,128)(2,1)} %pooling_w.1) | copy-start | bytes 393220
  17.5 52.7 %copy-start.5 = (bf16[256,256]{1,0:T(8,128)(2,1)S(1)}, bf16[256,256]{1,0:T(8,128)(2,1)}, u32[]{:S(2)}) copy-start(bf16[256,256]{1,0:T(8,128)(2,1)} %sender_w.3) | copy-start | bytes 393220
  17.5 52.7 %copy-start.6 = (bf16[256,256]{1,0:T(8,128)(2,1)S(1)}, bf16[256,256]{1,0:T(8,128)(2,1)}, u32[]{:S(2)}) copy-start(bf16[256,256]{1,0:T(8,128)(2,1)} %target_w.3) | copy-start | bytes 393220
  17.5 52.7 %copy-start.7 = (bf16[256,256]{1,0:T(8,128)(2,1)S(1)}, bf16[256,256]{1,0:T(8,128)(2,1)}, u32[]{:S(2)}) copy-start(bf16[256,256]{1,0:T(8,128)(2,1)} %update_w.3) | copy-start | bytes 393220
  17.5 52.7 %copy-start.8 = (bf16[256,256]{1,0:T(8,128)(2,1)S(1)}, bf16[256,256]{1,0:T(8,128)(2,1)}, u32[]{:S(2)}) copy-start(bf16[256,256]{1,0:T(8,128)(2,1)} %lifting_w.1) | copy-start | bytes 393220
  17.5 52.7 %copy-start.9 = (s32[4,512]{1,0:T(4,128)S(1)}, s32[4,512]{1,0:T(4,128)}, u32[]{:S(2)}) copy-start(s32[4,512]{1,0:T(4,128)} %reshape.26.window_ref) | copy-start | bytes 24580
  17.5 52.7 %copy-start.10 = (bf16[32,256]{1,0:T(8,128)(2,1)S(1)}, bf16[32,256]{1,0:T(8,128)(2,1)}, u32[]{:S(2)}) copy-start(bf16[32,256]{1,0:T(8,128)(2,1)} %latents_ref.1) | copy-start | bytes 49156
  70.2 1.2 %copy-start.1 = (bf16[2048,256]{1,0:T(8,128)(2,1)S(1)}, bf16[2048,256]{1,0:T(8,128)(2,1)}, u32[]{:S(2)}) copy-start(bf16[2048,256]{1,0:T(8,128)(2,1)} %get-tuple-element.5.refined_ref) | copy-start | bytes 3145732
  71.4 0.9 copy-start.2

commit v3 on v2

--- a/solution.py
+++ b/solution.py
@@ -7,8 +7,8 @@
 from jax.experimental.pallas import tpu as pltpu
 from jax.sharding import PartitionSpec as P
 
-EDGE_TILE = 512
-NODE_TILE = 512
+EDGE_TILE = 1024
+NODE_TILE = 1024
 F32 = jnp.float32
 BF16 = jnp.bfloat16
 
@@ -20,7 +20,7 @@
 
 
 def silu(values):
-    return values * pl.reciprocal(1.0 + jnp.exp(-values), approx=False)
+    return values * (0.5 + 0.5 * jnp.tanh(0.5 * values))
 
 
 def mm(a, b):
@@ -43,6 +43,13 @@
     spread = jnp.broadcast_to(row - first, (height, count)).astype(jnp.int16)
     place = lax.broadcasted_iota(jnp.int32, (height, count), 0).astype(jnp.int16)
     return jnp.where(spread == place, jnp.ones((height, count), BF16), jnp.zeros((height, count), BF16))
+
+
+def in_window(clusters, block):
+    within = clusters - lax.axis_index("region") * block
+    own = (within >= 0) & (within < block)
+    half = lax.axis_size("region") // 2 * block
+    return jnp.where(own, within, block + within + jnp.where(within < 0, half, -half))
 
 
 def fine_kernel(
@@ -81,11 +88,12 @@
 
     @pl.when(step < edge_steps)
     def _():
-        s_row = senders_ref[pl.ds(step, 1)]
-        t_row = targets_ref[pl.ds(step, 1)]
+        here = pl.ds(pl.multiple_of(step * tile, tile), tile)
+        s_row = senders_ref[here].reshape(1, tile)
+        t_row = targets_ref[here].reshape(1, tile)
         pieces = hot_columns(s_row, extended) + hot_columns(t_row, nodes) + [edges_ref[...]]
         hidden = silu(mm(jnp.concatenate(pieces, axis=1), table[...])).astype(BF16)
-        messages[pl.ds(pl.multiple_of(step * tile, tile), tile)] = normalize(
+        messages[here] = normalize(
             mm(hidden, message_w[...])
         ).astype(BF16)
 
@@ -95,14 +103,19 @@
         first = pl.multiple_of(number * NODE_TILE, NODE_TILE)
         here = pl.ds(first, NODE_TILE)
         hot = jnp.concatenate(
-            [hot_rows(targets_ref[k : k + 1], first, NODE_TILE) for k in range(edge_steps)], axis=1
+            [
+                hot_rows(targets_ref[pl.ds(k * tile, tile)].reshape(1, tile), first, NODE_TILE)
+                for k in range(edge_steps)
+            ],
+            axis=1,
         )
         inflow = mm(hot, messages[...]).astype(BF16)
         own = fine_ref[here]
         node_hidden = silu(mm(own, self_w[...]) + mm(inflow, inflow_w[...])).astype(BF16)
         refined = (own.astype(F32) + normalize(mm(node_hidden, update_w[...]))).astype(BF16)
         refined_ref[here] = refined
-        pooled[...] += mm(hot_rows(window_ref[pl.ds(number, 1)], 0, pooled.shape[0]), refined)
+        slots = in_window(window_ref[here].reshape(1, NODE_TILE), pooled.shape[0] // 2)
+        pooled[...] += mm(hot_rows(slots, 0, pooled.shape[0]), refined)
 
     @pl.when(step == pl.num_programs(0) - 1)
     def _():
@@ -144,9 +157,9 @@
         fine,
         halo,
         edges,
-        senders.reshape(edge_steps, EDGE_TILE),
-        targets.reshape(edge_steps, EDGE_TILE),
-        window_ids.reshape(node_steps, NODE_TILE),
+        senders,
+        targets,
+        window_ids,
         *weights,
     )
 
@@ -170,8 +183,8 @@
         pl.semaphore_signal(
             barrier, inc=1, device_id=(region, other), device_id_type=pl.DeviceIdType.MESH
         )
-    width = rows_ref.shape[1] // 2
-    hot = jnp.concatenate(hot_columns(rows_ref[...], fine_ref.shape[0]), axis=1)
+    width = rows_ref.shape[0] // 2
+    hot = jnp.concatenate(hot_columns(rows_ref[...].reshape(1, -1), fine_ref.shape[0]), axis=1)
     exported[...] = mm(hot, fine_ref[...]).astype(BF16)
     pl.semaphore_wait(barrier, 2)
     lower, upper = pl.ds(0, width), pl.ds(width, width)
@@ -205,7 +218,7 @@
         compiler_params=pltpu.CompilerParams(
             collective_id=0, has_side_effects=True, vmem_limit_bytes=32 * 2**20
         ),
-    )(fine, send_rows.reshape(1, -1))
+    )(fine, send_rows)
 
 
 def coarse_kernel(
@@ -283,12 +296,15 @@
             )
     for copy in pool:
         copy.start()
-    picked[...] = jnp.concatenate(hot_columns(senders_ref[...], block), axis=1)
-    for n in range(window_ref.shape[0]):
-        chosen[pl.ds(n * NODE_TILE, NODE_TILE)] = jnp.concatenate(
-            hot_columns(window_ref[n : n + 1], 2 * block), axis=1
-        )
-    target_row = hot_rows(targets_ref[...], 0, owned)
+    count = senders_ref.shape[0]
+    sender_row = senders_ref[...].reshape(1, count) - region * block
+    target_row = targets_ref[...].reshape(1, count) - (region * doms + me) * owned
+    picked[...] = jnp.concatenate(hot_columns(sender_row, block), axis=1)
+    for n in range(window_ref.shape[0] // NODE_TILE):
+        rows = pl.ds(n * NODE_TILE, NODE_TILE)
+        slots = in_window(window_ref[rows].reshape(1, NODE_TILE), block)
+        chosen[rows] = jnp.concatenate(hot_columns(slots, 2 * block), axis=1)
+    target_row = hot_rows(target_row, 0, owned)
     total = partial_ref[part(me)].astype(F32)
     for copy in pool:
         copy.wait_recv()
@@ -340,7 +356,7 @@
         copy.wait_send()
     for copy in lifts:
         copy.wait_recv()
-    for n in range(window_ref.shape[0]):
+    for n in range(window_ref.shape[0] // NODE_TILE):
         rows = pl.ds(n * NODE_TILE, NODE_TILE)
         fine_ref[rows] = (
             refined_ref[rows].astype(F32) + mm(chosen[rows], lifted[...])
@@ -379,9 +395,9 @@
         partial,
         refined,
         latents,
-        senders.reshape(1, -1),
-        targets.reshape(1, -1),
-        window_ids.reshape(-1, NODE_TILE),
+        senders,
+        targets,
+        window_ids,
         *weights,
     )
 
@@ -409,22 +425,18 @@
     upper_update,
     lifting_weight,
 ):
-    region_index = lax.axis_index("region")
-    dom_index = lax.axis_index("dom")
     dom_count = lax.axis_size("dom")
     region_count = lax.axis_size("region")
     owned = coarse_latents.shape[0]
     block = dom_count * owned
     halo = halo_stage(fine_latents, send_rows, dom_count)
-    is_partner = (cluster_ids // block != region_index).astype(jnp.int32)
-    window_ids = cluster_ids % block + is_partner * block
     refined, partial = fine_stage(
         fine_latents,
         halo,
         edge_latents,
         edge_senders,
         edge_targets,
-        window_ids,
+        cluster_ids,
         2 * block,
         (
             sender_weight,
@@ -440,9 +452,9 @@
         partial,
         refined,
         coarse_latents,
-        coarse_senders - region_index * block,
-        coarse_targets - (region_index * dom_count + dom_index) * owned,
-        window_ids,
+        coarse_senders,
+        coarse_targets,
+        cluster_ids,
         (pooling_weight, upper_sender, upper_target, upper_update, lifting_weight),
         region_count,
         dom_count,

time: 99.8 us -> 87.8 us (0.88)
  Pallas kernels: 86.8 us -> 80.4 us
  local copies, waits for them, and re-layouts: 9.71 us -> 6.34 us
  other arithmetic: 2.08 us -> 0 us
    pallas_call x1, Pallas kernels: 52.6 us -> 46.3 us  [fine_stage(): pl.pallas_call(functools.partial(fine_kernel, edge_steps), grid=(edge_ste...]
    reshape x3 -> x0, local copies, waits for them, and re-layouts: 3.38 us -> none  [the longest x1 1.39 us: fine_stage(): targets.reshape(edge_steps, EDGE_TILE)]
    sub x2 -> x0, other arithmetic: 1.37 us -> none  [the longest x1 0.69 us: body(): coarse_senders - region_index * block]
    unnamed x26 -> x30, local copies, waits for them, and re-layouts: 6.33 us -> 6.34 us
where the time goes in v3:
time: 87.8 us; the launch traced here: 87.5 us
  Pallas kernels  80.4 us (92%)
  local copies, waits for them, and re-layouts  6.34 us (7%)
    pallas_call x1, Pallas kernels, fine_stage(): pl.pallas_call(functools.partial(fine_kernel, edge_steps), grid=(edge_ste...  46.3 us
    pallas_call x1, Pallas kernels, coarse_stage(): pl.pallas_call(functools.partial(coarse_kernel, regions, doms), out_shape...  25.3 us
    pallas_call x1, Pallas kernels, halo_stage(): pl.pallas_call(functools.partial(halo_kernel, doms), out_shape=jax.ShapeD...  8.8 us
    unnamed x30, local copies, waits for them, and re-layouts  6.34 us

profile of v3, /device:TPU:0, one launch (start us, length us, event | category | flops | bytes accessed | tf_op | source)
XLA Modules:
  0.0 87.5 jit_solution(17358783525548113387)
XLA Ops:
  0.6 0.0 copy-start
  0.6 1.2 %copy-done = bf16[2048,256]{1,0:T(8,128)(2,1)S(1)} copy-done((bf16[2048,256]{1,0:T(8,128)(2,1)S(1)}, bf16[2048,256]{1,0:T(8,128)(2,1)}, u32[]{:S(2)}) %copy-start) | copy-done | bytes 1048600
  1.9 0.7 copy-done.13
  2.5 8.8 %shard_map.212.halo_ref = bf16[256,256]{1,0:T(8,128)(2,1)S(1)} custom-call(bf16[2048,256]{1,0:T(8,128)(2,1)S(1)} %copy-done, s32[256]{0:T(256)S(1)} %copy-done.13), custom_call_target="tpu_custom_call" | custom-call | tf_op jit(solution)/shard_map/pallas_call | solution.py:207
  11.4 0.6 copy-done.3
  12.0 0.0 copy-start.8
  12.0 0.0 copy-start.9
  12.0 0.0 copy-start.10
  12.0 0.0 copy-start.11
  12.1 0.0 copy-start.12
  12.1 46.3 %shard_map.213 = (bf16[2048,256]{1,0:T(8,128)(2,1)}, bf16[512,256]{1,0:T(8,128)(2,1)}) custom-call(bf16[2048,256]{1,0:T(8,128)(2,1)} %fine_ref.3, bf16[256,256]{1,0:T(8,128)(2,1)} %copy-done.3, bf16[9216,256]{1,0:T(8,128)(2,1)} %edges_ref.1, s32[9216]{0:T(1024)} %senders_ref.2, s32[9216]{0:T(1024)} %targets_ref.2, s32[2048]{0:T(1024)} %window_ref.3, ...), custom_call_target="tpu_custom_call" | custom-call | flops 32614907904 | bytes 8388608 | tf_op jit(solution)/shard_map/pallas_call | solution.py:131
  58.4 0.0 copy-done.5
  58.4 0.0 copy-done.6
  58.4 0.0 copy-done.7
  58.4 0.0 copy-done.8
  58.4 0.0 copy-done.9
  58.4 0.0 copy-done.10
  58.4 0.0 copy-done.11
  58.4 0.0 copy-start.1
  58.5 1.2 %copy-done.1 = bf16[2048,256]{1,0:T(8,128)(2,1)S(1)} copy-done((bf16[2048,256]{1,0:T(8,128)(2,1)S(1)}, bf16[2048,256]{1,0:T(8,128)(2,1)}, u32[]{:S(2)}) %copy-start.1) | copy-done | bytes 1048600
  59.7 0.9 %copy-done.2 = bf16[512,256]{1,0:T(8,128)(2,1)S(1)} copy-done((bf16[512,256]{1,0:T(8,128)(2,1)S(1)}, bf16[512,256]{1,0:T(8,128)(2,1)}, u32[]{:S(2)}) %copy-start.2) | copy-done | bytes 262168
  60.6 25.3 %shard_map.214 = (bf16[2048,256]{1,0:T(8,128)(2,1)S(1)}, bf16[32,256]{1,0:T(8,128)(2,1)S(1)}) custom-call(bf16[512,256]{1,0:T(8,128)(2,1)S(1)} %copy-done.2, bf16[2048,256]{1,0:T(8,128)(2,1)S(1)} %copy-done.1, bf16[32,256]{1,0:T(8,128)(2,1)S(1)} %copy-done.9, s32[512]{0:T(512)S(1)} %copy-done.11, s32[512]{0:T(512)S(1)} %copy-done.12, s32[2048]{0:T(1024)S(1)} %copy-done.10, ...), custom_call_target="tpu_custom_call" | custom-call | tf_op jit(solution)/shard_map/pallas_call | solution.py:375
  86.0 1.0 %copy.25 = bf16[2048,256]{1,0:T(8,128)(2,1)} copy(bf16[2048,256]{1,0:T(8,128)(2,1)S(1)} %get-tuple-element.8) | data formatting | bytes 2097152
  86.9 0.6 copy.26
  (9 shorter events, 0.0 us)
Async XLA Ops:
  0.6 1.2 %copy-start = (bf16[2048,256]{1,0:T(8,128)(2,1)S(1)}, bf16[2048,256]{1,0:T(8,128)(2,1)}, u32[]{:S(2)}) copy-start(bf16[2048,256]{1,0:T(8,128)(2,1)} %fine_ref.3) | copy-start | bytes 3145732
  1.9 0.7 copy-start.13
  11.3 0.7 copy-start.3
  12.0 46.4 %copy-start.4 = (bf16[256,256]{1,0:T(8,128)(2,1)S(1)}, bf16[256,256]{1,0:T(8,128)(2,1)}, u32[]{:S(2)}) copy-start(bf16[256,256]{1,0:T(8,128)(2,1)} %pooling_w.1) | copy-start | bytes 393220
  12.0 46.4 %copy-start.5 = (bf16[256,256]{1,0:T(8,128)(2,1)S(1)}, bf16[256,256]{1,0:T(8,128)(2,1)}, u32[]{:S(2)}) copy-start(bf16[256,256]{1,0:T(8,128)(2,1)} %sender_w.3) | copy-start | bytes 393220
  12.0 46.4 %copy-start.6 = (bf16[256,256]{1,0:T(8,128)(2,1)S(1)}, bf16[256,256]{1,0:T(8,128)(2,1)}, u32[]{:S(2)}) copy-start(bf16[256,256]{1,0:T(8,128)(2,1)} %target_w.3) | copy-start | bytes 393220
  12.0 46.4 %copy-start.7 = (bf16[256,256]{1,0:T(8,128)(2,1)S(1)}, bf16[256,256]{1,0:T(8,128)(2,1)}, u32[]{:S(2)}) copy-start(bf16[256,256]{1,0:T(8,128)(2,1)} %update_w.3) | copy-start | bytes 393220
  12.0 46.4 %copy-start.8 = (bf16[256,256]{1,0:T(8,128)(2,1)S(1)}, bf16[256,256]{1,0:T(8,128)(2,1)}, u32[]{:S(2)}) copy-start(bf16[256,256]{1,0:T(8,128)(2,1)} %lifting_w.1) | copy-start | bytes 393220
  12.0 46.4 %copy-start.9 = (bf16[32,256]{1,0:T(8,128)(2,1)S(1)}, bf16[32,256]{1,0:T(8,128)(2,1)}, u32[]{:S(2)}) copy-start(bf16[32,256]{1,0:T(8,128)(2,1)} %latents_ref.1) | copy-start | bytes 49156
  12.0 46.4 %copy-start.10 = (s32[2048]{0:T(1024)S(1)}, s32[2048]{0:T(1024)}, u32[]{:S(2)}) copy-start(s32[2048]{0:T(1024)} %window_ref.3) | copy-start | bytes 24580
  12.0 46.4 %copy-start.11 = (s32[512]{0:T(512)S(1)}, s32[512]{0:T(512)}, u32[]{:S(2)}) copy-start(s32[512]{0:T(512)} %senders_ref.3) | copy-start | bytes 6148
  12.1 46.4 %copy-start.12 = (s32[512]{0:T(512)S(1)}, s32[512]{0:T(512)}, u32[]{:S(2)}) copy-start(s32[512]{0:T(512)} %targets_ref.3) | copy-start | bytes 6148
  58.4 1.2 %copy-start.1 = (bf16[2048,256]{1,0:T(8,128)(2,1)S(1)}, bf16[2048,256]{1,0:T(8,128)(2,1)}, u32[]{:S(2)}) copy-start(bf16[2048,256]{1,0:T(8,128)(2,1)} %get-tuple-element.5.refined_ref) | copy-start | bytes 3145732
  59.7 0.9 %copy-start.2 = (bf16[512,256]{1,0:T(8,128)(2,1)S(1)}, bf16[512,256]{1,0:T(8,128)(2,1)}, u32[]{:S(2)}) copy-start(bf16[512,256]{1,0:T(8,128)(2,1)} %get-tuple-element.4.partial_ref) | copy-start | bytes 786436

commit v4 on v3

--- a/solution.py
+++ b/solution.py
@@ -216,7 +216,7 @@
             pltpu.SemaphoreType.DMA((2,)),
         ],
         compiler_params=pltpu.CompilerParams(
-            collective_id=0, has_side_effects=True, vmem_limit_bytes=32 * 2**20
+            collective_id=0, has_side_effects=True, vmem_limit_bytes=60 * 2**20
         ),
     )(fine, send_rows)
 
@@ -248,9 +248,13 @@
     from_recv,
     lift_send,
     lift_recv,
+    kept,
+    kept_sem,
 ):
     region, me = lax.axis_index("region"), lax.axis_index("dom")
     partner = lax.rem(region + regions // 2, regions)
+    keep = pltpu.make_async_copy(refined_ref, kept, kept_sem)
+    keep.start()
     owned = latents_ref.shape[0]
     block = doms * owned
 
@@ -354,12 +358,13 @@
         copy.start()
     for copy in pool + shares:
         copy.wait_send()
+    keep.wait()
     for copy in lifts:
         copy.wait_recv()
     for n in range(window_ref.shape[0] // NODE_TILE):
         rows = pl.ds(n * NODE_TILE, NODE_TILE)
         fine_ref[rows] = (
-            refined_ref[rows].astype(F32) + mm(chosen[rows], lifted[...])
+            kept[rows].astype(F32) + mm(chosen[rows], lifted[...])
         ).astype(BF16)
     for copy in lifts:
         copy.wait_send()
@@ -378,7 +383,7 @@
             jax.ShapeDtypeStruct((nodes, depth), BF16),
             jax.ShapeDtypeStruct((owned, depth), BF16),
         ),
-        in_specs=[whole] * 11,
+        in_specs=[whole, pl.BlockSpec(memory_space=pl.ANY)] + [whole] * 9,
         out_specs=(whole, whole),
         scratch_shapes=[
             pltpu.VMEM((2 * doms, owned, depth), BF16),
@@ -387,9 +392,10 @@
             pltpu.VMEM((nodes, 2 * block), BF16),
             pltpu.VMEM((count, block), BF16),
         ]
-        + pair * 3,
+        + pair * 3
+        + [pltpu.VMEM((nodes, depth), BF16), pltpu.SemaphoreType.DMA],
         compiler_params=pltpu.CompilerParams(
-            collective_id=1, has_side_effects=True, vmem_limit_bytes=48 * 2**20
+            collective_id=1, has_side_effects=True, vmem_limit_bytes=60 * 2**20
         ),
     )(
         partial,

time: 87.8 us -> 88.9 us (1.013)
  Pallas kernels: 80.4 us -> 84.4 us
  local copies, waits for them, and re-layouts: 6.34 us -> 3.59 us
    unnamed x30 -> x2, local copies, waits for them, and re-layouts: 6.34 us -> 3.59 us
    pallas_call x1, Pallas kernels: 25.3 us -> 27.6 us  [coarse_stage(): pl.pallas_call(functools.partial(coarse_kernel, regions, doms), out_shape...]
    pallas_call x1, Pallas kernels: 8.8 us -> 10.7 us  [halo_stage(): pl.pallas_call(functools.partial(halo_kernel, doms), out_shape=jax.ShapeD...]
where the time goes in v4:
time: 88.9 us; the launch traced here: 88.7 us
  Pallas kernels  84.4 us (95%)
  local copies, waits for them, and re-layouts  3.59 us (4%)
    pallas_call x1, Pallas kernels, fine_stage(): pl.pallas_call(functools.partial(fine_kernel, edge_steps), grid=(edge_ste...  46.2 us
    pallas_call x1, Pallas kernels, coarse_stage(): pl.pallas_call(functools.partial(coarse_kernel, regions, doms), out_shape...  27.6 us
    pallas_call x1, Pallas kernels, halo_stage(): pl.pallas_call(functools.partial(halo_kernel, doms), out_shape=jax.ShapeD...  10.7 us
    unnamed x2, local copies, waits for them, and re-layouts  3.59 us

profile of v4, /device:TPU:0, one launch (start us, length us, event | category | flops | bytes accessed | tf_op | source)
XLA Modules:
  0.0 88.7 jit_solution(18163165458832504443)
XLA Ops:
  0.6 10.7 %shard_map.212.halo_ref = bf16[256,256]{1,0:T(8,128)(2,1)} custom-call(bf16[2048,256]{1,0:T(8,128)(2,1)} %fine_ref.3, s32[256]{0:T(256)} %rows_ref.1), custom_call_target="tpu_custom_call" | custom-call | tf_op jit(solution)/shard_map/pallas_call | solution.py:207
  11.3 46.2 %shard_map.213 = (bf16[2048,256]{1,0:T(8,128)(2,1)}, bf16[512,256]{1,0:T(8,128)(2,1)}) custom-call(bf16[2048,256]{1,0:T(8,128)(2,1)} %fine_ref.3, bf16[256,256]{1,0:T(8,128)(2,1)} %shard_map.212.halo_ref, bf16[9216,256]{1,0:T(8,128)(2,1)} %edges_ref.1, s32[9216]{0:T(1024)} %senders_ref.2, s32[9216]{0:T(1024)} %targets_ref.2, s32[2048]{0:T(1024)} %window_ref.3, ...), custom_call_target="tpu_custom_call" | custom-call | flops 32614907904 | bytes 8388608 | tf_op jit(solution)/shard_map/pallas_call | solution.py:131
  57.5 27.6 %shard_map.214 = (bf16[2048,256]{1,0:T(8,128)(2,1)}, bf16[32,256]{1,0:T(8,128)(2,1)}) custom-call(bf16[512,256]{1,0:T(8,128)(2,1)} %get-tuple-element.4.partial_ref, bf16[2048,256]{1,0:T(8,128)(2,1)} %get-tuple-element.5.refined_ref, bf16[32,256]{1,0:T(8,128)(2,1)} %latents_ref.1, s32[512]{0:T(512)} %senders_ref.3, s32[512]{0:T(512)} %targets_ref.3, ...), custom_call_target="tpu_custom_call" | custom-call | tf_op jit(solution)/shard_map/pallas_call | solution.py:380
  85.1 2.3 %copy.25 = bf16[2048,256]{1,0:T(8,128)(2,1)} copy(bf16[2048,256]{1,0:T(8,128)(2,1)} %get-tuple-element.8) | data formatting | bytes 2097152
  87.3 1.3 %copy.26 = bf16[32,256]{1,0:T(8,128)(2,1)} copy(bf16[32,256]{1,0:T(8,128)(2,1)} %get-tuple-element.9) | data formatting | bytes 32768
